TPU v7x, 256 devices: a whole 4x4x8 slice. The times are simulated.
256 devices in a mesh: list: 64 (over z_lo, y, x, core), row: 4 (over z_hi).
Axes of the slice: x: 4, y: 4, z: 8 (z_hi: 4, z_lo: 2; z = z_hi * 2 + z_lo), core: 2. Of those that a mesh axis runs over, the one named last changes fastest.
Arguments:
- corpus: bfloat16 [262144, 768], P(('list', 'row')), may hold values from -6 to 6
- row_list: int32 [262144], P(('list', 'row')), may hold values from 0 to 4095, as said below
- list_slot: int32 [4096], replicated, may hold values from 0 to 4095, as said below
- member_counts: int32 [4096], P('list'), may hold values from 32 to 96, as said below
- old_centroids: float32 [4096, 768], P('list'), may hold values from -6 to 6
- next_rows: bfloat16 [393216, 768], P(('list', 'row')), may hold values from -6 to 6
Outputs:
- new_centroids: float32 [4096, 768], P('list')
- best_score: float32 [393216], P(('list', 'row'))
Inputs may be any that keep to these rules, and one draw needn't show every extreme that they name: `row_list`: each device sends every owner (list_slot // 64) at least 8 and at most 24 of its rows; some owner receives 24 rows from every device. `list_slot`: A permutation of the list numbers. `member_counts`: the exact number of corpus rows in each slot's list; the lists of one owner differ by at most one.
All inputs are finite; a program needn't handle non-finite values.
Results may differ from a plain program's by a relative error of at most 0.0025.
Values may be sent and summed in bfloat16 or wider, within the bound.
A program may use at most 64 MiB of HBM per device.

v0:
```python
import jax
import jax.numpy as jnp
from jax import lax
from jax.sharding import PartitionSpec as P

ITERS = 3


eps_norm = 1e-06
aniso_par = 32.0
perp_weight = 1.0
prior_weight = 16.0


def unit_of(row_block):
    values = row_block.astype(jnp.float32)
    scaled = values / jnp.sqrt(jnp.sum(values * values, axis=1, keepdims=True) + eps_norm)
    return scaled.astype(jnp.bfloat16)


def split_pair(values):
    high_part = values.astype(jnp.bfloat16)
    low_part = (values - high_part.astype(jnp.float32)).astype(jnp.bfloat16)
    return (high_part, low_part)


def prepare(member_block, member_local, lists_own):
    unit_rows = unit_of(member_block)
    membership = (member_local[:, None] == jnp.arange(lists_own, dtype=jnp.int32)[None, :]).astype(
        jnp.float32
    )
    return (unit_rows, membership)


def gram_part(unit_rows, membership, vectors):
    inner_dims = (((1,), (1,)), ((), ()))
    outer_dims = (((0,), (0,)), ((), ()))
    vec_high, vec_low = split_pair(vectors)
    scores = lax.dot_general(unit_rows, vec_high, inner_dims, preferred_element_type=jnp.float32)
    scores = scores + lax.dot_general(
        unit_rows, vec_low, inner_dims, preferred_element_type=jnp.float32
    )
    weighted = scores * membership
    wgt_high, wgt_low = split_pair(weighted)
    result = lax.dot_general(wgt_high, unit_rows, outer_dims, preferred_element_type=jnp.float32)
    return result + lax.dot_general(
        wgt_low, unit_rows, outer_dims, preferred_element_type=jnp.float32
    )


def member_total(membership, member_block):
    return lax.dot_general(
        membership.astype(jnp.bfloat16),
        member_block,
        (((0,), (0,)), ((), ())),
        preferred_element_type=jnp.float32,
    )


def on_device(corpus, row_list, list_slot, member_counts, old_centroids, next_rows):
    n_owner = lax.axis_size("list")
    lists_own = old_centroids.shape[0]
    local_rows = corpus.shape[0]
    cap_slots = 3 * local_rows // (2 * n_owner)
    width = corpus.shape[1]
    slot_ids = jnp.take(list_slot, row_list)
    owner_id = slot_ids // lists_own
    local_id = slot_ids % lists_own
    hits = (owner_id[:, None] == jnp.arange(n_owner, dtype=jnp.int32)[None, :]).astype(jnp.int32)
    rank_in = jnp.sum((jnp.cumsum(hits, axis=0) - 1) * hits, axis=1)
    dest_idx = owner_id * cap_slots + rank_in
    send_rows = (
        jnp.zeros((n_owner * cap_slots, width), jnp.bfloat16)
        .at[dest_idx]
        .set(corpus)
        .reshape(n_owner, cap_slots, width)
    )
    send_local = (
        jnp.full((n_owner * cap_slots,), -1, jnp.int32)
        .at[dest_idx]
        .set(local_id)
        .reshape(n_owner, cap_slots)
    )
    recv_rows, recv_local = (
        lax.all_to_all(send_rows, "list", split_axis=0, concat_axis=0, tiled=True),
        lax.all_to_all(send_local, "list", split_axis=0, concat_axis=0, tiled=True),
    )
    recv_rows = recv_rows.reshape(n_owner * cap_slots, width)
    recv_local = recv_local.reshape(n_owner * cap_slots)
    centroids = old_centroids
    unit_rows, membership = prepare(recv_rows, recv_local, lists_own)
    row_sums, first_gram = lax.psum(
        (member_total(membership, recv_rows), gram_part(unit_rows, membership, centroids)), "row"
    )
    diag_term = perp_weight * member_counts.astype(jnp.float32)[:, None] + prior_weight
    residual = (
        aniso_par * row_sums
        + prior_weight * centroids
        - (diag_term * centroids + (aniso_par - perp_weight) * first_gram)
    )
    direction = residual
    norm_now = jnp.sum(residual * residual, axis=1, keepdims=True)
    for iteration in range(ITERS):
        applied = diag_term * direction + (aniso_par - perp_weight) * lax.psum(
            gram_part(unit_rows, membership, direction), "row"
        )
        step_len = norm_now / jnp.sum(direction * applied, axis=1, keepdims=True)
        centroids = centroids + step_len * direction
        residual = residual - step_len * applied
        norm_next = jnp.sum(residual * residual, axis=1, keepdims=True)
        direction = residual + norm_next / norm_now * direction
        norm_now = norm_next
    panel = centroids.astype(jnp.bfloat16)
    start_score = jnp.full((next_rows.shape[0],), -jnp.inf, jnp.float32)
    piece = lax.all_gather(panel, "list", axis=0, tiled=True)
    piece_rows = piece.shape[0]
    block_size = 512
    blocks = piece.reshape(piece_rows // block_size, block_size, piece.shape[1])

    def one_block(running, piece_block):
        scores = lax.dot_general(
            next_rows, piece_block, (((1,), (1,)), ((), ())), preferred_element_type=jnp.float32
        )
        return (jnp.maximum(running, jnp.max(scores, axis=1)), None)

    result, unused = lax.scan(one_block, start_score, blocks)
    return (centroids, result / width)


def solution(mesh):
    in_specs = (
        P(("list", "row"), None),
        P(("list", "row")),
        P(),
        P("list"),
        P("list", None),
        P(("list", "row"), None),
    )
    out_specs = (P("list", None), P(("list", "row")))
    return jax.shard_map(
        on_device, mesh=mesh, in_specs=in_specs, out_specs=out_specs, check_vma=False
    )
```

profile of v0, /device:TPU:1, one launch (start us, length us, event | category | flops | bytes accessed | tf_op | source)
XLA Modules:
  0.0 470.4 jit_solution(17790374509922220616)
XLA Ops:
  7.2 0.8 fusion.41
  7.9 6.1 %gather_fusion = s32[1024]{0:T(1024)S(1)} fusion(s32[4096]{0:T(1024)S(1)} %copy-done, s32[1024]{0:T(1024)S(1)} %fusion.41), kind=kCustom, calls=%fused_computation | custom fusion | bytes 12288 | tf_op jit(solution)/shard_map/jit(_take)/gather | solution.py:66
  14.2 18.0 %reduce-window.6 = s32[64,8,128]{2,1,0:T(8,128)S(1)} reduce-window(s32[64,8,128]{2,1,0:T(8,128)S(1)} %fusion.11, s32[]{:T(128)} %constant.69.clone.1), window={size=1x1x128 pad=0_0x0_0x127_0}, to_apply=%region_0.1 | reduce-window | flops 8323072 | bytes 524292 | tf_op jit(solution)/shard_map/reduce-window
  32.8 4.3 scatter_custom_fusion
  37.1 0.7 all_to_all.9
  37.8 10.3 %all-to-all-start = ((s32[64,1,24]{2,1,0:T(1,128)}), s32[64,1,24]{2,1,0:T(1,128)S(1)}, u32[]{:S(2)}, u32[]{:S(2)}) async-start(s32[64,1,24]{2,1,0:T(1,128)} %bitcast.3), calls=%async_computation | async-start | bytes 65536 | tf_op jit(solution)/shard_map/all_to_all | solution.py:86
  48.2 7.5 %scatter_custom_fusion.1 = bf16[1536,768]{1,0:T(8,128)(2,1)} fusion(s32[1024]{0:T(1024)S(1)} %compare_select_fusion, bf16[1024,768]{1,0:T(8,128)(2,1)} %param.8, bf16[]{:T(256)} %constant.79.clone.1), kind=kCustom, calls=%fused_computation.18 | custom fusion | bytes 2359808 | tf_op jit(solution)/shard_map/scatter | solution.py:75
  55.9 8.6 %all-to-all-start.1 = ((bf16[64,24,768]{2,1,0:T(8,128)(2,1)}), bf16[64,24,768]{2,1,0:T(8,128)(2,1)S(1)}, u32[]{:S(2)}, u32[]{:S(2)}) async-start(bf16[64,24,768]{2,1,0:T(8,128)(2,1)} %bitcast.46), calls=%async_computation.1 | async-start | bytes 4718592 | tf_op jit(solution)/shard_map/all_to_all | solution.py:85
  65.1 0.7 reduce.5
  65.9 29.0 %all-to-all-done.1 = bf16[64,24,768]{2,1,0:T(8,128)(2,1)S(1)} async-done(((bf16[64,24,768]{2,1,0:T(8,128)(2,1)}), bf16[64,24,768]{2,1,0:T(8,128)(2,1)S(1)}, u32[]{:S(2)}, u32[]{:S(2)}) %all-to-all-start.1) | async-done | bytes 2359328 | tf_op jit(solution)/shard_map/all_to_all | solution.py:85
  95.5 0.9 copy-done.1
  96.5 2.2 divide_convert_fusion
  98.7 0.8 fusion.36
  99.5 0.8 fusion.6
  100.9 1.2 convolution_add_fusion.7
  102.1 1.2 fusion.12
  103.6 52.9 %all-reduce.12.cloned.1.call-done = (f32[64,768]{1,0:T(8,128)}, f32[64,768]{1,0:T(8,128)}) async-done(((f32[64,768]{1,0:T(8,128)}, f32[64,768]{1,0:T(8,128)}), (f32[64,768]{1,0:T(8,128)}, f32[64,768]{1,0:T(8,128)})) %all-reduce.12.cloned.1.call-update) | async-done | bytes 393232 | tf_op jit(solution)/shard_map/psum | solution.py:92
  156.4 1.1 add_subtract_fusion
  157.6 0.8 fusion.33
  158.4 0.8 fusion.5
  159.7 1.2 convolution_add_fusion.6
  161.0 49.5 %all-reduce.6.cloned.1.call-done = f32[64,768]{1,0:T(8,128)} async-done(((f32[64,768]{1,0:T(8,128)}), f32[64,768]{1,0:T(8,128)}) %all-reduce.6.cloned.1.call-update) | async-done | bytes 196624 | tf_op jit(solution)/shard_map/psum | solution.py:104
  210.5 1.1 multiply_reduce_fusion.5
  211.7 1.1 multiply_reduce_fusion.4
  212.9 0.8 fusion.30
  213.8 0.8 fusion.4
  215.1 1.2 convolution_add_fusion.5
  216.4 49.2 %all-reduce.8.cloned.1.call-done = f32[64,768]{1,0:T(8,128)} async-done(((f32[64,768]{1,0:T(8,128)}), f32[64,768]{1,0:T(8,128)}) %all-reduce.8.cloned.1.call-update) | async-done | bytes 196624 | tf_op jit(solution)/shard_map/psum | solution.py:104
  265.6 1.1 multiply_reduce_fusion.3
  266.8 1.1 multiply_reduce_fusion.2
  267.9 1.1 multiply_add_fusion.1
  269.0 0.8 fusion.27
  269.8 0.8 fusion.3
  271.2 1.2 convolution_add_fusion.4
  272.5 49.3 %all-reduce.10.cloned.1.call-done = f32[64,768]{1,0:T(8,128)} async-done(((f32[64,768]{1,0:T(8,128)}), f32[64,768]{1,0:T(8,128)}) %all-reduce.10.cloned.1.call-update) | async-done | bytes 196624 | tf_op jit(solution)/shard_map/psum | solution.py:104
  321.8 1.1 multiply_reduce_fusion.1
  322.9 0.8 fusion.43
  323.7 112.5 %all-gather.2.cloned.1.call-done = bf16[4096,768]{1,0:T(8,128)(2,1)} async-done(((bf16[64,768]{1,0:T(8,128)(2,1)}), bf16[4096,768]{1,0:T(8,128)(2,1)}) %all-gather.2.cloned.1.call-update) | async-done | bytes 6291472 | tf_op jit(solution)/shard_map/all_gather | solution.py:115
  436.2 27.1 %while.11 = (s32[]{:T(128)}, f32[1536]{0:T(1024)S(1)}, bf16[8,512,768]{2,1,0:T(8,128)(2,1)}, bf16[1536,768]{1,0:T(8,128)(2,1)}, s32[]{:T(128)}, /*index=5*/s32[]{:T(128)}) while((s32[]{:T(128)}, f32[1536]{0:T(1024)S(1)}, bf16[8,512,768]{2,1,0:T(8,128)(2,1)}, bf16[1536,768]{1,0:T(8,128)(2,1)}, s32[]{:T(128)}, ...), condition=%wide.region_19.20_spmd.clone, body=%wide.region_17.19_spmd.clone.sunk | while | flops 1208747520 | bytes 3170895 | solution.py:126
  436.2 3.3 convolution_reduce_fusion.2
  439.6 3.3 convolution_reduce_fusion.2
  443.0 3.3 convolution_reduce_fusion.2
  446.4 3.3 convolution_reduce_fusion.2
  449.8 3.3 convolution_reduce_fusion.2
  453.2 3.3 convolution_reduce_fusion.2
  456.5 3.3 convolution_reduce_fusion.2
  459.9 3.3 convolution_reduce_fusion.2
  463.3 0.6 broadcast_multiply_fusion
  (57 shorter events, 4.9 us)
Async XLA Ops:
  7.2 0.8 copy-start
  7.2 6.9 %copy-start.4 = (s32[1024]{0:T(1024)S(1)}, s32[1024]{0:T(1024)}, u32[]{:S(2)}) copy-start(s32[1024]{0:T(1024)} %param.9) | copy-start | bytes 12292
  37.8 18.1 %all-to-all-start = ((s32[64,1,24]{2,1,0:T(1,128)}), s32[64,1,24]{2,1,0:T(1,128)S(1)}, u32[]{:S(2)}, u32[]{:S(2)}) async-start(s32[64,1,24]{2,1,0:T(1,128)} %bitcast.3), calls=%async_computation | async-start | bytes 65536 | tf_op jit(solution)/shard_map/all_to_all | solution.py:86
  55.9 39.0 %all-to-all-start.1 = ((bf16[64,24,768]{2,1,0:T(8,128)(2,1)}), bf16[64,24,768]{2,1,0:T(8,128)(2,1)S(1)}, u32[]{:S(2)}, u32[]{:S(2)}) async-start(bf16[64,24,768]{2,1,0:T(8,128)(2,1)} %bitcast.46), calls=%async_computation.1 | async-start | bytes 4718592 | tf_op jit(solution)/shard_map/all_to_all | solution.py:85
  64.6 91.9 %all-reduce.12.cloned.1.call-start = ((), (), s32[]{:S(2)}) async-start(), calls=%async_computation.6 | async-start | bytes 786432 | tf_op jit(solution)/shard_map/psum | solution.py:92
  95.0 1.4 copy-start.1
  96.5 2.2 copy-start.3
  100.4 1.7 copy-start.2
  100.9 2.7 copy-start.5
  103.3 107.2 %all-reduce.6.cloned.1.call-start = ((), (), s32[]{:S(2)}) async-start(), calls=%async_computation.2 | async-start | bytes 393216 | tf_op jit(solution)/shard_map/psum | solution.py:104
  161.0 104.7 %all-reduce.8.cloned.1.call-start = ((), (), s32[]{:S(2)}) async-start(), calls=%async_computation.3 | async-start | bytes 393216 | tf_op jit(solution)/shard_map/psum | solution.py:104
  216.3 105.4 %all-reduce.10.cloned.1.call-start = ((), (), s32[]{:S(2)}) async-start(), calls=%async_computation.4 | async-start | bytes 393216 | tf_op jit(solution)/shard_map/psum | solution.py:104
  272.4 163.8 %all-gather.2.cloned.1.call-start = ((), (), s32[]{:S(2)}) async-start(), calls=%async_computation.5 | async-start | bytes 6389760 | tf_op jit(solution)/shard_map/all_gather | solution.py:115
Sparse Core Ops, SparseCore 0:
  103.5 52.9 all-reduce.11
  161.1 49.3 all-reduce.5
  216.5 49.1 all-reduce.7
  272.5 49.1 all-reduce.9
  323.9 112.3 all-gather.1
where the time goes:
time: 471 us; the launch traced here: 470 us
  waiting for transfers between devices  343 us (73%)
  matrix products  41.5 us (9%)
  other arithmetic  31.9 us (7%)
  local copies, waits for them, and re-layouts  20.6 us (4%)
  starting transfers between devices  19.3 us (4%)
  between operations  14.1 us (3%)
    psum x3, waiting for transfers between devices, on_device(): lax.psum(gram_part(unit_rows, membership, direction), 'row')  148 us
    all_gather x1, waiting for transfers between devices, on_device(): piece = lax.all_gather(panel, 'list', axis=0, tiled=True)  112 us
    psum x1, waiting for transfers between devices, on_device(): lax.psum((member_total(membership, recv_rows), gram_part(unit_rows, membe...  52.9 us
    all_to_all x1, waiting for transfers between devices, on_device(): lax.all_to_all(send_rows, 'list', split_axis=0, concat_axis=0, tiled=True)  29 us
    dot_general x8, matrix products, one_block(): lax.dot_general(next_rows, piece_block, (((1,), (1,)), ((), ())), preferr...  26.8 us
    another operation x2, other arithmetic  18 us
    all_to_all x1, starting transfers between devices, on_device(): lax.all_to_all(send_local, 'list', split_axis=0, concat_axis=0, tiled=True)  10.3 us
  transfers between devices with their start and end apart: 7, of which 7 were waited for; matrix products, arithmetic and copies ran while one was open for 2% of the time, Pallas kernels for 0%

commit v1 on v0

v1 whole, which is shorter than its diff:
```python
import jax
import jax.numpy as jnp
from jax import lax
from jax.experimental import pallas as pl
from jax.experimental.pallas import tpu as pltpu
from jax.sharding import PartitionSpec as P

MESH = pl.DeviceIdType.MESH
F32 = jnp.float32
BF16 = jnp.bfloat16
I32 = jnp.int32

ITERS = 3
N_LIST = 64
N_ROW = 4
LO = 64
D = 768
H = D // 2
ROWS_DEV = 1024
NEXT_DEV = 1536
CAP = 24
CAP2 = 2 * CAP
GROUP = 16
QUARTER = LO // N_ROW
SHARDS = 32

eps_norm = 1e-06
aniso_par = 32.0
perp_weight = 1.0
prior_weight = 16.0
gram_weight = aniso_par - perp_weight


def nt(a, b):
    return lax.dot_general(a, b, (((1,), (1,)), ((), ())), preferred_element_type=F32)


def nn(a, b):
    return lax.dot_general(a, b, (((1,), (0,)), ((), ())), preferred_element_type=F32)


def split_pair(values):
    high_part = values.astype(BF16)
    low_part = (values - high_part.astype(F32)).astype(BF16)
    return high_part, low_part


def iota(shape, dim):
    return lax.broadcasted_iota(I32, shape, dim)


def wait_for(ref, sem):
    pltpu.make_async_copy(ref, ref, sem).wait()


def kernel(
    corpus, row_list, list_slot, counts, old, next_hbm,
    out_cent, out_best,
    key, ids_send, send, ids_recv, recv, unit, member,
    first, first_in, gram_all, direction, grams, grams_in, dots, dots_in,
    diag, pan, next_all, best, best_in,
    a2a_send, a2a_recv, ids_send_sem, ids_recv_sem,
    next_sem, first_sem, dir_sem, gram_sem, dot_sem, cent_sem,
    z_sem, one_sem, two_sem, two_recv, best_sem,
):
    l = lax.axis_index("list")
    r = lax.axis_index("row")
    c = l % 2
    x = (l // 2) % 4
    y = (l // 8) % 4
    zl = l // 32

    def list_of(zl_, y_, x_, c_):
        return ((zl_ * 4 + y_) * 4 + x_) * 2 + c_

    mine = (y - x + 4) % 4
    place = mine * GROUP + zl * 8 + x * 2 + c

    def list_at(group, member_):
        zl_ = member_ // 8
        x_ = (member_ // 2) % 4
        return list_of(zl_, (x_ + group) % 4, x_, member_ % 2)

    barrier = pltpu.get_barrier_semaphore()

    def greet(k, carry):
        pl.semaphore_signal(
            barrier, inc=1, device_id={"list": (l + k) % N_LIST, "row": r}, device_id_type=MESH
        )
        return carry

    lax.fori_loop(1, N_LIST, greet, 0)
    for k in range(1, N_ROW):
        for z_ in range(2):
            pl.semaphore_signal(
                barrier,
                inc=1,
                device_id={"list": list_of((zl + z_) % 2, y, x, c), "row": (r + k) % N_ROW},
                device_id_type=MESH,
            )

    own_next = pltpu.make_async_copy(next_hbm, next_all.at[c], next_sem.at[0])
    own_next.start()

    ids_row = row_list[...]
    table = list_slot[...]
    table2 = jnp.concatenate([(table // LO) * LO, table % LO], axis=0).astype(F32)
    high = ids_row // 128
    low = ids_row % 128
    pick = (iota((32, ROWS_DEV), 0) == high).astype(F32)
    pick2 = jnp.concatenate([pick, pick], axis=0).astype(BF16)
    looked = nn(table2.T.astype(BF16), pick2)
    slot = jnp.sum(
        jnp.where(iota((128, ROWS_DEV), 0) == low, looked, 0.0), axis=0, keepdims=True
    ).astype(I32)
    owner = slot // LO
    local = slot % LO
    oc = owner % 2
    ox = (owner // 2) % 4
    oy = (owner // 8) % 4
    oz = owner // 32
    spot = ((oy - ox + 4) % 4) * GROUP + oz * 8 + ox * 2 + oc
    hit = iota((N_LIST, ROWS_DEV), 0) == spot
    hits = hit.astype(F32)
    before = (iota((256, 256), 0) < iota((256, 256), 1)).astype(F32).astype(BF16)
    carry = jnp.zeros((N_LIST, 1), F32)
    ranks = []
    for b in range(ROWS_DEV // 256):
        part = hits[:, b * 256 : (b + 1) * 256]
        ranks.append(nn(part.astype(BF16), before) + carry)
        carry = carry + jnp.sum(part, axis=1, keepdims=True)
    rank = jnp.concatenate(ranks, axis=1)
    key[...] = jnp.where(hit, rank, -1.0).astype(I32)
    rank_row = jnp.sum(hits * rank, axis=0, keepdims=True).astype(I32)
    named = (hits * (local + 1).astype(F32)).astype(BF16)
    at_rank = (iota((128, ROWS_DEV), 0) == rank_row).astype(F32).astype(BF16)
    ids_send[...] = nt(named, at_rank) - 1.0

    pl.semaphore_wait(barrier, N_LIST - 1 + 2 * (N_ROW - 1))

    def send_group(chunk, carry_):
        group = (mine + chunk) % 4
        keys = key[pl.ds(pl.multiple_of(group * GROUP, GROUP), GROUP), :]
        chosen = keys.reshape(GROUP, 1, ROWS_DEV) == iota((GROUP, CAP, ROWS_DEV), 1)
        chosen = chosen.astype(F32).reshape(GROUP * CAP, ROWS_DEV).astype(BF16)
        rows = nn(chosen, corpus[...]).reshape(GROUP, CAP, D)
        rows = jnp.concatenate([rows[:, :, :H], rows[:, :, H:]], axis=1)
        send[pl.ds(pl.multiple_of(group * GROUP * CAP2, GROUP * CAP2), GROUP * CAP2), :] = (
            rows.reshape(GROUP * CAP2, H).astype(BF16)
        )

        def send_one(j, carry2):
            m = (place % GROUP + j) % GROUP
            to = group * GROUP + m

            @pl.when(to != place)
            def _():
                device = {"list": list_at(group, m), "row": r}
                pltpu.make_async_remote_copy(
                    src_ref=ids_send.at[pl.ds(to, 1)],
                    dst_ref=ids_recv.at[pl.ds(place, 1)],
                    send_sem=ids_send_sem,
                    recv_sem=ids_recv_sem.at[chunk],
                    device_id=device,
                    device_id_type=MESH,
                ).start()
                pltpu.make_async_remote_copy(
                    src_ref=send.at[pl.ds(pl.multiple_of(to * CAP2, CAP2), CAP2)],
                    dst_ref=recv.at[pl.ds(pl.multiple_of(place * CAP2, CAP2), CAP2)],
                    send_sem=a2a_send,
                    recv_sem=a2a_recv.at[chunk],
                    device_id=device,
                    device_id_type=MESH,
                ).start()

            return carry2

        lax.fori_loop(0, GROUP, send_one, 0)
        return carry_

    lax.fori_loop(0, 4, send_group, 0)
    own_block = pl.ds(pl.multiple_of(place * CAP2, CAP2), CAP2)
    recv[own_block, :] = send[own_block, :]
    ids_recv[pl.ds(place, 1), :] = ids_send[pl.ds(place, 1), :]

    other_core = {"list": list_of(zl, y, x, 1 - c), "row": r}
    swap = pltpu.make_async_remote_copy(
        src_ref=next_hbm,
        dst_ref=next_all.at[c],
        send_sem=next_sem.at[1],
        recv_sem=next_sem.at[2],
        device_id=other_core,
        device_id_type=MESH,
    )
    swap.start()

    count_row = counts[...].astype(F32)
    square = iota((LO, LO), 0) == iota((LO, LO), 1)
    count_col = jnp.sum(jnp.where(square, count_row, 0.0), axis=1, keepdims=True)
    diag[...] = jnp.broadcast_to(perp_weight * count_col + prior_weight, (LO, 128))

    old_high, old_low = split_pair(old[...])
    old_two = jnp.concatenate([old_high, old_low], axis=0)
    width = GROUP * CAP
    source_of = (iota((GROUP, width), 1) * 2731) // 65536
    lane = iota((128, width), 1)
    spread = (lane - ((lane * 2731) // 65536) * CAP == iota((128, width), 0)).astype(F32).astype(BF16)
    first[...] = jnp.zeros_like(first)

    def take_group(chunk, carry_):
        group = (mine - chunk + 4) % 4

        @pl.when(chunk == 0)
        def _():
            wait_for(ids_recv.at[pl.ds(0, GROUP - 1)], ids_recv_sem.at[0])
            wait_for(recv.at[pl.ds(0, (GROUP - 1) * CAP2)], a2a_recv.at[0])

        @pl.when(chunk > 0)
        def _():
            wait_for(ids_recv.at[pl.ds(0, GROUP)], ids_recv_sem.at[chunk])
            wait_for(recv.at[pl.ds(0, GROUP * CAP2)], a2a_recv.at[chunk])

        named_in = ids_recv[pl.ds(pl.multiple_of(group * GROUP, GROUP), GROUP), :]
        wide = nn(named_in.astype(BF16), spread)
        flat = jnp.sum(
            jnp.where(source_of == iota((GROUP, width), 0), wide, 0.0), axis=0, keepdims=True
        ).astype(I32)
        own = (iota((LO, width), 0) == flat).astype(F32)
        member[:, pl.ds(pl.multiple_of(group * width, width), width)] = own
        raw = recv[pl.ds(pl.multiple_of(group * GROUP * CAP2, GROUP * CAP2), GROUP * CAP2), :]
        raw = raw.astype(F32).reshape(GROUP, CAP2, H)
        rows = jnp.concatenate(
            [raw[:, :CAP, :].reshape(width, H), raw[:, CAP:, :].reshape(width, H)], axis=1
        )
        inverse = lax.rsqrt(jnp.sum(rows * rows, axis=1, keepdims=True) + eps_norm)
        units = (rows * inverse).astype(BF16)
        unit[pl.ds(pl.multiple_of(group * width, width), width), :] = units
        scores = nt(old_two, units)
        scores = (scores[:LO] + scores[LO:]) * own * (-gram_weight)
        wgt_high, wgt_low = split_pair(scores)
        first[...] += (
            nn((own * aniso_par).astype(BF16), rows.astype(BF16))
            + nn(wgt_high, units)
            + nn(wgt_low, units)
        )
        return carry_

    lax.fori_loop(0, 4, take_group, 0)

    quarter = pl.ds(pl.multiple_of(r * QUARTER, QUARTER), QUARTER)

    def peer(k):
        return (r + k) % N_ROW

    def rows_of(k):
        return pl.ds(pl.multiple_of(peer(k) * QUARTER, QUARTER), QUARTER)

    def scatter(source, target, send_sem, recv_sem):
        for k in (1, 3, 2):
            pltpu.make_async_remote_copy(
                src_ref=source.at[rows_of(k)],
                dst_ref=target.at[quarter],
                send_sem=send_sem,
                recv_sem=recv_sem,
                device_id={"list": l, "row": peer(k)},
                device_id_type=MESH,
            ).start()

    def gather(ref, send_sem, recv_sem):
        for k in (1, 3, 2):
            pltpu.make_async_remote_copy(
                src_ref=ref.at[quarter],
                dst_ref=ref.at[quarter],
                send_sem=send_sem,
                recv_sem=recv_sem,
                device_id={"list": l, "row": peer(k)},
                device_id_type=MESH,
            ).start()

    three = pl.ds(0, 3 * QUARTER)
    scatter(first, first_in, first_sem.at[0], first_sem.at[1])
    wait_for(first_in.at[three], first_sem.at[1])
    old_own = old[quarter, :]
    diag_own = diag[quarter, :][:, :1]
    residual = first[quarter, :] + (prior_weight - diag_own) * old_own
    for k in range(1, N_ROW):
        residual = residual + first_in[rows_of(k), :]
    centroid = old_own
    moved = residual
    norm_now = jnp.sum(residual * residual, axis=1, keepdims=True)
    for step in range(ITERS):
        dir_now = direction.at[step]
        dir_now[quarter, :] = moved.astype(BF16)
        moved = moved.astype(BF16).astype(F32)
        gather(dir_now, dir_sem.at[2 * step], dir_sem.at[2 * step + 1])
        wait_for(dir_now.at[three], dir_sem.at[2 * step + 1])
        scores = nt(dir_now[...], unit[...]) * member[...]
        if step < ITERS - 1:
            gram = nn(scores.astype(BF16), unit[...])
            grams[step] = gram.astype(BF16)
            gram_all[...] = gram
            scatter(
                grams.at[step], grams_in.at[step], gram_sem.at[2 * step], gram_sem.at[2 * step + 1]
            )
            wait_for(grams_in.at[step].at[three], gram_sem.at[2 * step + 1])
            total = gram_all[quarter, :]
            for k in range(1, N_ROW):
                total = total + grams_in.at[step][rows_of(k), :].astype(F32)
            applied = diag_own * moved + gram_weight * total
            step_len = norm_now / jnp.sum(moved * applied, axis=1, keepdims=True)
            centroid = centroid + step_len * moved
            residual = residual - step_len * applied
            norm_next = jnp.sum(residual * residual, axis=1, keepdims=True)
            moved = residual + norm_next / norm_now * moved
            norm_now = norm_next
        else:
            squares = jnp.sum(scores * scores, axis=1, keepdims=True)
            dots[...] = jnp.broadcast_to(squares, (LO, 128))
            scatter(dots, dots_in, dot_sem.at[0], dot_sem.at[1])
            wait_for(dots_in.at[three], dot_sem.at[1])
            total = dots[quarter, :]
            for k in range(1, N_ROW):
                total = total + dots_in[rows_of(k), :]
            bend = diag_own * jnp.sum(moved * moved, axis=1, keepdims=True)
            step_len = norm_now / (bend + gram_weight * total[:, :1])
            centroid = centroid + step_len * moved

    a_own = (y * 4 + x) * LO
    b_own = (16 + x * 4 + y) * LO
    pan_own = (1 - zl) * a_own + zl * b_own
    piece = pl.ds(pl.multiple_of(pan_own + r * QUARTER, QUARTER), QUARTER)
    pan[piece, :] = centroid.astype(BF16)
    for k in range(N_ROW):
        for z_ in range(2):
            if k == 0 and z_ == 0:
                continue
            pltpu.make_async_remote_copy(
                src_ref=pan.at[piece],
                dst_ref=pan.at[piece],
                send_sem=z_sem.at[0],
                recv_sem=z_sem.at[1],
                device_id={"list": list_of((zl + z_) % 2, y, x, c), "row": peer(k)},
                device_id_type=MESH,
            ).start()
    out_cent[quarter, :] = centroid
    wait_for(pan.at[pl.ds(0, 7 * QUARTER)], z_sem.at[1])

    def at(start, n):
        return pl.ds(pl.multiple_of(start, LO), n)

    for k in (1, 3, 2):
        for half, start, device in (
            (0, a_own, list_of(zl, y, (x + k) % 4, c)),
            (1, b_own, list_of(zl, (y + k) % 4, x, c)),
        ):
            pltpu.make_async_remote_copy(
                src_ref=pan.at[at(start, LO)],
                dst_ref=pan.at[at(start, LO)],
                send_sem=one_sem.at[half],
                recv_sem=one_sem.at[2 + half],
                device_id={"list": device, "row": r},
                device_id_type=MESH,
            ).start()
    own_next.wait()
    swap.wait_recv()
    for half in range(2):
        wait_for(pan.at[pl.ds(0, 3 * LO)], one_sem.at[2 + half])
    a_four = y * 4 * LO
    b_four = (16 + x * 4) * LO
    for k in (1, 3, 2):
        for half, start, device in (
            (0, a_four, list_of(zl, (y + k) % 4, x, c)),
            (1, b_four, list_of(zl, y, (x + k) % 4, c)),
        ):
            pltpu.make_async_remote_copy(
                src_ref=pan.at[at(start, 4 * LO)],
                dst_ref=pan.at[at(start, 4 * LO)],
                send_sem=two_sem.at[half],
                recv_sem=two_recv.at[half * 4 + k],
                device_id={"list": device, "row": r},
                device_id_type=MESH,
            ).start()
    gather(out_cent, cent_sem.at[0], cent_sem.at[1])

    best[...] = jnp.full_like(best, -jnp.inf)

    def score_chunk(step, carry_):
        half = step % 2
        order = step // 2
        dist = order + (order == 2).astype(I32) - (order == 3).astype(I32)
        spot_ = (1 - half) * y + half * x
        start = half * 16 * LO + ((spot_ - dist + 4) % 4) * 4 * LO

        @pl.when(order > 0)
        def _():
            wait_for(pan.at[pl.ds(0, 4 * LO)], two_recv.at[half * 4 + dist])

        block = pan[pl.ds(pl.multiple_of(start, 4 * LO), 4 * LO), :]

        for core in range(2):
            for b in range(NEXT_DEV // 512):
                found = nt(block, next_all[core, b * 512 : (b + 1) * 512, :])
                top = jnp.max(found.reshape(4 * LO // 8, 8, 512), axis=0)
                lanes = slice(b * 512, (b + 1) * 512)
                best[core, :, lanes] = jnp.maximum(best[core, :, lanes], top)
        return carry_

    lax.fori_loop(0, 8, score_chunk, 0)

    top_other = jnp.max(best[1 - c], axis=0, keepdims=True)
    best_in[0] = top_other
    back = pltpu.make_async_remote_copy(
        src_ref=best_in.at[0],
        dst_ref=best_in.at[1],
        send_sem=best_sem.at[0],
        recv_sem=best_sem.at[1],
        device_id=other_core,
        device_id_type=MESH,
    )
    back.start()
    top_own = jnp.max(best[c], axis=0, keepdims=True)
    wait_for(out_cent.at[three], cent_sem.at[1])

    wait_for(ids_send.at[pl.ds(0, N_LIST - 1)], ids_send_sem)
    wait_for(send.at[pl.ds(0, (N_LIST - 1) * CAP2)], a2a_send)
    swap.wait_send()
    wait_for(first.at[three], first_sem.at[0])
    for step in range(ITERS):
        wait_for(direction.at[step].at[three], dir_sem.at[2 * step])
    for step in range(ITERS - 1):
        wait_for(grams.at[step].at[three], gram_sem.at[2 * step])
    wait_for(dots.at[three], dot_sem.at[0])
    wait_for(pan.at[pl.ds(0, 7 * QUARTER)], z_sem.at[0])
    for half in range(2):
        wait_for(pan.at[pl.ds(0, 3 * LO)], one_sem.at[half])
        wait_for(pan.at[pl.ds(0, 12 * LO)], two_sem.at[half])
    wait_for(out_cent.at[three], cent_sem.at[0])
    back.wait()
    out_best[...] = jnp.maximum(top_own, best_in[1]) / D


def on_device(corpus, row_list, list_slot, member_counts, old_centroids, next_rows):
    vmem = pl.BlockSpec(memory_space=pltpu.VMEM)
    dma = pltpu.SemaphoreType.DMA
    cent, best = pl.pallas_call(
        kernel,
        out_shape=(
            jax.ShapeDtypeStruct((LO, D), F32),
            jax.ShapeDtypeStruct((1, NEXT_DEV), F32),
        ),
        in_specs=[vmem] * 5 + [pl.BlockSpec(memory_space=pl.ANY)],
        out_specs=(vmem, vmem),
        scratch_shapes=[
            pltpu.VMEM((N_LIST, ROWS_DEV), I32),
            pltpu.VMEM((N_LIST, 128), F32),
            pltpu.VMEM((N_LIST * CAP2, H), BF16),
            pltpu.VMEM((N_LIST, 128), F32),
            pltpu.VMEM((N_LIST * CAP2, H), BF16),
            pltpu.VMEM((N_LIST * CAP, D), BF16),
            pltpu.VMEM((LO, N_LIST * CAP), F32),
            pltpu.VMEM((LO, D), F32),
            pltpu.VMEM((LO, D), F32),
            pltpu.VMEM((LO, D), F32),
            pltpu.VMEM((ITERS, LO, D), BF16),
            pltpu.VMEM((ITERS - 1, LO, D), BF16),
            pltpu.VMEM((ITERS - 1, LO, D), BF16),
            pltpu.VMEM((LO, 128), F32),
            pltpu.VMEM((LO, 128), F32),
            pltpu.VMEM((LO, 128), F32),
            pltpu.VMEM((SHARDS * LO, D), BF16),
            pltpu.VMEM((2, NEXT_DEV, D), BF16),
            pltpu.VMEM((2, 8, NEXT_DEV), F32),
            pltpu.VMEM((2, 1, NEXT_DEV), F32),
            dma, dma((4,)), dma, dma((4,)),
            dma((3,)), dma((2,)), dma((2 * ITERS,)), dma((2 * ITERS - 2,)), dma((2,)), dma((2,)),
            dma((2,)), dma((4,)), dma((2,)), dma((8,)), dma((2,)),
        ],
        compiler_params=pltpu.CompilerParams(
            collective_id=0, has_side_effects=True, vmem_limit_bytes=56 * 2**20
        ),
    )(
        corpus,
        row_list.reshape(1, ROWS_DEV),
        list_slot.reshape(32, 128),
        member_counts.reshape(1, LO),
        old_centroids,
        next_rows,
    )
    return cent, best.reshape(NEXT_DEV)


def solution(mesh):
    in_specs = (
        P(("list", "row"), None),
        P(("list", "row")),
        P(),
        P("list"),
        P("list", None),
        P(("list", "row"), None),
    )
    out_specs = (P("list", None), P(("list", "row")))
    return jax.shard_map(
        on_device, mesh=mesh, in_specs=in_specs, out_specs=out_specs, check_vma=False
    )
```

time: 471 us -> 131 us (0.28)
  waiting for transfers between devices: 343 us -> 0 us
  Pallas kernels: 0 us -> 127 us
  matrix products: 41.5 us -> 0 us
  other arithmetic: 31.9 us -> 1.31 us
  starting transfers between devices: 19.3 us -> 0 us
  local copies, waits for them, and re-layouts: 20.6 us -> 1.62 us
  between operations: 14.1 us -> 0.64 us
    psum x4 -> x0, waiting for transfers between devices: 201 us -> none  [the longest x3 148 us: on_device(): lax.psum(gram_part(unit_rows, membership, direction), 'row')]
    pallas_call x0 -> x1, Pallas kernels: none -> 127 us  [on_device(): pl.pallas_call(kernel, out_shape=(jax.ShapeDtypeStruct((LO, D), F32), jax...]
    all_gather x1 -> x0, waiting for transfers between devices: 112 us -> none  [on_device(): piece = lax.all_gather(panel, 'list', axis=0, tiled=True)]
    dot_general x25 -> x0, matrix products: 41.5 us -> none  [the longest x8 26.8 us: one_block(): lax.dot_general(next_rows, piece_block, (((1,), (1,)), ((), ())), preferr...]
    all_to_all x2 -> x0, waiting for transfers between devices: 29.3 us -> none  [the longest x1 29 us: on_device(): lax.all_to_all(send_rows, 'list', split_axis=0, concat_axis=0, tiled=True)]
    all_to_all x2 -> x0, starting transfers between devices: 19 us -> none  [the longest x1 10.3 us: on_device(): lax.all_to_all(send_local, 'list', split_axis=0, concat_axis=0, tiled=True)]
    another operation x2 -> x0, other arithmetic: 18 us -> none
    scatter x2 -> x0, local copies, waits for them, and re-layouts: 11.8 us -> none  [the longest x1 7.47 us: on_device(): send_rows = jnp.zeros((n_owner * cap_slots, width), jnp.bfloat16).at[dest...]
  transfers between devices with their start and end apart: 7 -> 0, of which waited for: 7 -> 0; matrix products, arithmetic and copies ran while one was open for 2% -> 0% of each run, Pallas kernels for 0% -> 0%
where the time goes in v1:
time: 131 us
  Pallas kernels  127 us (97%)
  local copies, waits for them, and re-layouts  1.62 us (1%)
  other arithmetic  1.31 us (1%)
    pallas_call x1, Pallas kernels, on_device(): pl.pallas_call(kernel, out_shape=(jax.ShapeDtypeStruct((LO, D), F32), jax...  127 us

profile of v1, /device:TPU:1, one launch (start us, length us, event | category | flops | bytes accessed | tf_op | source)
XLA Modules:
  0.0 130.8 jit_solution(13577438491881224442)
XLA Ops:
  0.6 127.2 %shard_map.77 = (f32[64,768]{1,0:T(8,128)}, f32[1,1536]{1,0:T(1,128)}) custom-call(bf16[1024,768]{1,0:T(8,128)(2,1)} %corpus.1, s32[1,1024]{1,0:T(1,128)} %bitcast.4, s32[32,128]{1,0:T(8,128)} %bitcast.3, s32[1,64]{1,0:T(1,128)} %bitcast.5, f32[64,768]{1,0:T(8,128)} %old.1, bf16[1536,768]{1,0:T(8,128)(2,1)} %next_hbm.1), custom_call_target="tpu_custom_call" | custom-call | tf_op jit(solution)/shard_map/pallas_call | solution.py:445
  127.8 1.3 %reduce = f32[1536]{0:T(1024)} reduce(f32[1,1536]{1,0:T(1,128)} %get-tuple-element.5, f32[]{:T(128)} %constant), dimensions={0}, to_apply=%get-tuple-element.5.reduce_sub_computation | reduce | bytes 12292 | tf_op jit(solution)/shard_map/pallas_call | solution.py:445
  129.2 1.6 %copy.9 = f32[64,768]{1,0:T(8,128)} copy(f32[64,768]{1,0:T(8,128)} %get-tuple-element.8) | data formatting | bytes 393216

commit v2 on v1

v2 whole, which is shorter than its diff:
```python
import itertools

import jax
import jax.numpy as jnp
from jax import lax
from jax.experimental import pallas as pl
from jax.experimental.pallas import tpu as pltpu
from jax.sharding import PartitionSpec as P

MESH = pl.DeviceIdType.MESH
F32 = jnp.float32
BF16 = jnp.bfloat16
I32 = jnp.int32

ITERS = 3
N_LIST = 64
N_ROW = 4
LO = 64
D = 768
H = D // 2
ROWS_DEV = 1024
NEXT_DEV = 1536
CAP = 24
CAP2 = 2 * CAP
GROUP = 16
QUARTER = LO // N_ROW
SHARDS = 16
HALF = NEXT_DEV // 2
PIECE = HALF // 2
AWAY = 6 * HALF
RING = (0, 1, 2, 1)
SEND_ORDER = (1, 3, 2, 0)
NEAR = AWAY + NEXT_DEV

eps_norm = 1e-06
aniso_par = 32.0
perp_weight = 1.0
prior_weight = 16.0
gram_weight = aniso_par - perp_weight


def nt(a, b):
    return lax.dot_general(a, b, (((1,), (1,)), ((), ())), preferred_element_type=F32)


def nn(a, b):
    return lax.dot_general(a, b, (((1,), (0,)), ((), ())), preferred_element_type=F32)


def split_pair(values):
    high_part = values.astype(BF16)
    low_part = (values - high_part.astype(F32)).astype(BF16)
    return high_part, low_part


def iota(shape, dim):
    return lax.broadcasted_iota(I32, shape, dim)


def wait_for(ref, sem):
    pltpu.make_async_copy(ref, ref, sem).wait()


def kernel(
    corpus_hbm, row_list, list_slot, counts, old, next_hbm,
    out_cent, out_best,
    corpus, key, ids_send, send, ids_recv, recv, unit, member,
    first, first_high, first_low, high_in, low_in, gram_all, direction, grams, grams_in,
    last, dots_in, diag, pan, nexts, best, best_in,
    corpus_sem, a2a_send, a2a_recv, ids_send_sem, ids_recv_sem,
    high_sem, low_sem, dir_sem, gram_sem, last_sem, dot_sem,
    next_sem, next_send, next_recv, pan_send, pan_recv, core_send, core_recv, best_sem,
):
    l = lax.axis_index("list")
    r = lax.axis_index("row")
    c = l % 2
    x = (l // 2) % 4
    y = (l // 8) % 4
    zl = l // 32

    def list_of(zl_, y_, x_, c_):
        return ((zl_ * 4 + y_) * 4 + x_) * 2 + c_

    mine = (y - x + 4) % 4
    place = mine * GROUP + zl * 8 + x * 2 + c

    z_part = [zl * 32, (1 - zl) * 32]
    y_part = [((y + k) % 4) * 8 for k in range(4)]
    x_at = [(x + k) % 4 for k in range(4)]
    c_at = [c, 1 - c]

    beyond = (r + 2 * zl - 1 + N_ROW) % N_ROW
    row_core = [r + (beyond - r) * c_at[k] for k in range(2)]
    row_from = [[r, r], row_core]
    row_to = [r, row_core[0]]

    def chip(dx, dy, dz=0):
        spot_ = list_of(zl if dz == 0 else 1 - zl, (y + dy + 4) % 4, (x + dx + 4) % 4, c)
        row = r if dz == 0 else (r + zl + (0 if dz > 0 else N_ROW - 1)) % N_ROW
        return {"list": spot_, "row": row}

    twos = ((0, 0), (2, 0), (0, 2), (2, 2))

    barrier = pltpu.get_barrier_semaphore()

    def greet_device(device):
        pl.semaphore_signal(barrier, inc=1, device_id=device, device_id_type=MESH)

    for k in (2, 1, 3):
        greet_device({"list": l, "row": (r + k) % N_ROW})
    for dx, dy in twos[::-1]:
        for dz in (1, -1):
            greet_device(chip(dx, dy, dz))
    offsets = itertools.product(range(4), range(4), range(2), range(2))
    for dy, dx, dz, dc in sorted(offsets, key=lambda o: -RING[o[0]] - RING[o[1]] - o[2]):
        if dy or dx or dz or dc:
            other = z_part[dz] + y_part[dy] + x_at[dx] * 2 + c_at[dc]
            greet_device({"list": other, "row": row_from[dz][dc]})

    own_corpus = pltpu.make_async_copy(corpus_hbm, corpus, corpus_sem)
    own_corpus.start()
    own_next = pltpu.make_async_copy(next_hbm, nexts.at[pl.ds(AWAY, NEXT_DEV)], next_sem)
    own_next.start()

    ids_row = row_list[...]
    table = list_slot[...]
    table2 = jnp.concatenate([(table // LO) * LO, table % LO], axis=0).astype(F32)
    high = ids_row // 128
    low = ids_row % 128
    pick = (iota((32, ROWS_DEV), 0) == high).astype(F32)
    pick2 = jnp.concatenate([pick, pick], axis=0).astype(BF16)
    looked = nn(table2.T.astype(BF16), pick2)
    slot = jnp.sum(
        jnp.where(iota((128, ROWS_DEV), 0) == low, looked, 0.0), axis=0, keepdims=True
    ).astype(I32)
    owner = slot // LO
    local = slot % LO
    oc = owner % 2
    ox = (owner // 2) % 4
    oy = (owner // 8) % 4
    oz = owner // 32
    spot = ((oy - ox + 4) % 4) * GROUP + oz * 8 + ox * 2 + oc
    hit = iota((N_LIST, ROWS_DEV), 0) == spot
    hits = hit.astype(F32)
    before = (iota((256, 256), 0) < iota((256, 256), 1)).astype(F32).astype(BF16)
    carry = jnp.zeros((N_LIST, 1), F32)
    ranks = []
    for b in range(ROWS_DEV // 256):
        part = hits[:, b * 256 : (b + 1) * 256]
        ranks.append(nn(part.astype(BF16), before) + carry)
        carry = carry + jnp.sum(part, axis=1, keepdims=True)
    rank = jnp.concatenate(ranks, axis=1)
    key[...] = jnp.where(hit, rank, -1.0).astype(I32)
    rank_row = jnp.sum(hits * rank, axis=0, keepdims=True).astype(I32)
    named = (hits * (local + 1).astype(F32)).astype(BF16)
    at_rank = (iota((128, ROWS_DEV), 0) == rank_row).astype(F32).astype(BF16)
    ids_send[...] = nt(named, at_rank) - 1.0

    own_corpus.wait()
    pl.semaphore_wait(barrier, N_LIST - 1 + N_ROW - 1 + 8)

    def send_group(chunk, carry_):
        group = (mine + chunk) % 4
        keys = key[pl.ds(pl.multiple_of(group * GROUP, GROUP), GROUP), :]
        chosen = keys.reshape(GROUP, 1, ROWS_DEV) == iota((GROUP, CAP, ROWS_DEV), 1)
        chosen = chosen.astype(F32).reshape(GROUP * CAP, ROWS_DEV).astype(BF16)
        rows = nn(chosen, corpus[...]).reshape(GROUP, CAP, D)
        rows = jnp.concatenate([rows[:, :, :H], rows[:, :, H:]], axis=1)
        send[pl.ds(pl.multiple_of(group * GROUP * CAP2, GROUP * CAP2), GROUP * CAP2), :] = (
            rows.reshape(GROUP * CAP2, H).astype(BF16)
        )

        def send_one(to, device):
            pltpu.make_async_remote_copy(
                src_ref=ids_send.at[pl.ds(to, 1)],
                dst_ref=ids_recv.at[pl.ds(place, 1)],
                send_sem=ids_send_sem,
                recv_sem=ids_recv_sem.at[chunk],
                device_id=device,
                device_id_type=MESH,
            ).start()
            pltpu.make_async_remote_copy(
                src_ref=send.at[pl.ds(pl.multiple_of(to * CAP2, CAP2), CAP2)],
                dst_ref=recv.at[pl.ds(pl.multiple_of(place * CAP2, CAP2), CAP2)],
                send_sem=a2a_send,
                recv_sem=a2a_recv.at[chunk],
                device_id=device,
                device_id_type=MESH,
            ).start()

        for dx in SEND_ORDER:
            y_part_ = ((y + dx + chunk) % 4) * 8
            for dz in (1, 0):
                for dc in range(2):
                    to = group * GROUP + z_part[dz] // 4 + x_at[dx] * 2 + c_at[dc]
                    device = {
                        "list": z_part[dz] + y_part_ + x_at[dx] * 2 + c_at[dc],
                        "row": row_to[dz],
                    }
                    if dx or dz or dc:
                        send_one(to, device)
                    else:
                        pl.when(chunk > 0)(lambda to=to, device=device: send_one(to, device))

        return carry_

    lax.fori_loop(0, 4, send_group, 0)
    own_block = pl.ds(pl.multiple_of(place * CAP2, CAP2), CAP2)
    recv[own_block, :] = send[own_block, :]
    ids_recv[pl.ds(place, 1), :] = ids_send[pl.ds(place, 1), :]

    count_row = counts[...].astype(F32)
    square = iota((LO, LO), 0) == iota((LO, LO), 1)
    count_col = jnp.sum(jnp.where(square, count_row, 0.0), axis=1, keepdims=True)
    diag[...] = jnp.broadcast_to(perp_weight * count_col + prior_weight, (LO, 128))

    def pass_on(start, to_set, part, device, at):
        pltpu.make_async_remote_copy(
            src_ref=nexts.at[pl.ds(start, PIECE)],
            dst_ref=nexts.at[pl.ds(to_set * HALF + part * PIECE, PIECE)],
            send_sem=next_send,
            recv_sem=next_recv.at[at],
            device_id=device,
            device_id_type=MESH,
        ).start()

    sides = ((1, 0), (-1, 0), (0, 1), (0, -1))

    old_high, old_low = split_pair(old[...])
    old_two = jnp.concatenate([old_high, old_low], axis=0)
    width = GROUP * CAP
    source_of = (iota((GROUP, width), 1) * 2731) // 65536
    lane = iota((128, width), 1)
    spread = (lane - ((lane * 2731) // 65536) * CAP == iota((128, width), 0)).astype(F32).astype(BF16)
    first[...] = jnp.zeros_like(first)

    def take_group(chunk, carry_):
        group = (mine - chunk + 4) % 4

        @pl.when(chunk == 0)
        def _():
            wait_for(ids_recv.at[pl.ds(0, GROUP - 1)], ids_recv_sem.at[0])
            wait_for(recv.at[pl.ds(0, (GROUP - 1) * CAP2)], a2a_recv.at[0])

        @pl.when(chunk > 0)
        def _():
            wait_for(ids_recv.at[pl.ds(0, GROUP)], ids_recv_sem.at[chunk])
            wait_for(recv.at[pl.ds(0, GROUP * CAP2)], a2a_recv.at[chunk])

        @pl.when(chunk == 3)
        def _():
            own_next.wait()
            for j, (dx, dy) in enumerate(sides):
                pass_on(AWAY + (j % 2) * HALF + (j // 2) * PIECE, j, j // 2, chip(dx, dy), j)

        named_in = ids_recv[pl.ds(pl.multiple_of(group * GROUP, GROUP), GROUP), :]
        wide = nn(named_in.astype(BF16), spread)
        flat = jnp.sum(
            jnp.where(source_of == iota((GROUP, width), 0), wide, 0.0), axis=0, keepdims=True
        ).astype(I32)
        own = (iota((LO, width), 0) == flat).astype(F32)
        member[:, pl.ds(pl.multiple_of(group * width, width), width)] = own
        raw = recv[pl.ds(pl.multiple_of(group * GROUP * CAP2, GROUP * CAP2), GROUP * CAP2), :]
        raw = raw.astype(F32).reshape(GROUP, CAP2, H)
        rows = jnp.concatenate(
            [raw[:, :CAP, :].reshape(width, H), raw[:, CAP:, :].reshape(width, H)], axis=1
        )
        inverse = lax.rsqrt(jnp.sum(rows * rows, axis=1, keepdims=True) + eps_norm)
        units = (rows * inverse).astype(BF16)
        unit[pl.ds(pl.multiple_of(group * width, width), width), :] = units
        scores = nt(old_two, units)
        scores = (scores[:LO] + scores[LO:]) * own * (-gram_weight)
        wgt_high, wgt_low = split_pair(scores)
        first[...] += (
            nn((own * aniso_par).astype(BF16), rows.astype(BF16))
            + nn(wgt_high, units)
            + nn(wgt_low, units)
        )
        return carry_

    lax.fori_loop(0, 4, take_group, 0)

    quarter = pl.ds(pl.multiple_of(r * QUARTER, QUARTER), QUARTER)

    def peer(k):
        return (r + k) % N_ROW

    def rows_of(k):
        return pl.ds(pl.multiple_of(peer(k) * QUARTER, QUARTER), QUARTER)

    def scatter(source, target, send_sem, recv_sem):
        for k in (1, 3, 2):
            pltpu.make_async_remote_copy(
                src_ref=source.at[rows_of(k)],
                dst_ref=target.at[quarter],
                send_sem=send_sem,
                recv_sem=recv_sem,
                device_id={"list": l, "row": peer(k)},
                device_id_type=MESH,
            ).start()

    def gather(ref, send_sem, recv_sem):
        for k in (1, 3, 2):
            pltpu.make_async_remote_copy(
                src_ref=ref.at[quarter],
                dst_ref=ref.at[quarter],
                send_sem=send_sem,
                recv_sem=recv_sem,
                device_id={"list": l, "row": peer(k)},
                device_id_type=MESH,
            ).start()

    three = pl.ds(0, 3 * QUARTER)

    def pass_more():
        for j in range(4):
            wait_for(nexts.at[pl.ds(0, PIECE)], next_recv.at[j])
        for j, (dx, dy) in enumerate(sides):
            part = j // 2
            over = chip(dy, dx)
            pass_on(j * HALF + part * PIECE, 4 + j % 2, part, over, 8 + j)
            pass_on(AWAY + (j % 2) * HALF + (1 - part) * PIECE, j, 1 - part, chip(dx, dy), 4 + j)

    high_part, low_part = split_pair(first[...])
    first_high[...] = high_part
    first_low[...] = low_part
    scatter(first_high, high_in, high_sem.at[0], high_sem.at[1])
    scatter(first_low, low_in, low_sem.at[0], low_sem.at[1])
    old_own = old[quarter, :]
    diag_own = diag[quarter, :][:, :1]
    residual = first[quarter, :] + (prior_weight - diag_own) * old_own
    wait_for(high_in.at[three], high_sem.at[1])
    for k in range(1, N_ROW):
        residual = residual + high_in[rows_of(k), :].astype(F32)
    centroid = old_own
    moved = residual
    for step in range(ITERS):
        dir_now = direction.at[step]
        dir_now[quarter, :] = moved.astype(BF16)
        moved = moved.astype(BF16).astype(F32)
        gather(dir_now, dir_sem.at[2 * step], dir_sem.at[2 * step + 1])
        if step == ITERS - 1:
            last[quarter, :D] = centroid
            last[quarter, D:] = jnp.broadcast_to(norm_now, (QUARTER, 128))
            gather(last, last_sem.at[0], last_sem.at[1])
        wait_for(dir_now.at[three], dir_sem.at[2 * step + 1])
        scores = nt(dir_now[...], unit[...]) * member[...]
        if step == ITERS - 1:
            break
        gram = nn(scores.astype(BF16), unit[...])
        grams[step] = gram.astype(BF16)
        gram_all[...] = gram
        scatter(
            grams.at[step], grams_in.at[step], gram_sem.at[2 * step], gram_sem.at[2 * step + 1]
        )
        if step == 0:
            pass_more()
            wait_for(low_in.at[three], low_sem.at[1])
            for k in range(1, N_ROW):
                residual = residual + low_in[rows_of(k), :].astype(F32)
            norm_now = jnp.sum(residual * residual, axis=1, keepdims=True)
        wait_for(grams_in.at[step].at[three], gram_sem.at[2 * step + 1])
        total = gram_all[quarter, :]
        for k in range(1, N_ROW):
            total = total + grams_in.at[step][rows_of(k), :].astype(F32)
        applied = diag_own * moved + gram_weight * total
        step_len = norm_now / jnp.sum(moved * applied, axis=1, keepdims=True)
        centroid = centroid + step_len * moved
        residual = residual - step_len * applied
        norm_next = jnp.sum(residual * residual, axis=1, keepdims=True)
        moved = residual + norm_next / norm_now * moved
        norm_now = norm_next

    squares = jnp.sum(scores * scores, axis=1, keepdims=True)
    squares = jnp.sum(jnp.where(square, squares, 0.0), axis=0, keepdims=True)
    dots_in[pl.ds(r, 1), :] = jnp.concatenate([squares, squares], axis=1)
    for k in (2, 1, 3):
        pltpu.make_async_remote_copy(
            src_ref=dots_in.at[pl.ds(r, 1)],
            dst_ref=dots_in.at[pl.ds(r, 1)],
            send_sem=dot_sem.at[0],
            recv_sem=dot_sem.at[1],
            device_id={"list": l, "row": peer(k)},
            device_id_type=MESH,
        ).start()
    moved = direction[ITERS - 1].astype(F32)
    bend = diag[...][:, :1] * jnp.sum(moved * moved, axis=1, keepdims=True)
    wait_for(last.at[three], last_sem.at[1])
    wait_for(dots_in.at[pl.ds(0, N_ROW - 1)], dot_sem.at[1])
    total = jnp.sum(dots_in[...], axis=0, keepdims=True)[:, :LO]
    total = jnp.sum(jnp.where(square, total, 0.0), axis=1, keepdims=True)
    step_len = last[:, D : D + 1] / (bend + gram_weight * total)
    centroid = last[:, :D] + step_len * moved

    own_rows = pl.ds(pl.multiple_of((c * 2 + zl) * LO, LO), LO)
    pan[own_rows, :] = centroid.astype(BF16)

    def push(j, part, n, device):
        pltpu.make_async_remote_copy(
            src_ref=pan.at[pl.ds(pl.multiple_of((c * 2 + zl) * LO + part * n, n), n)],
            dst_ref=pan.at[pl.ds(pl.multiple_of(((j * 2 + c) * 2 + zl) * LO + part * n, n), n)],
            send_sem=pan_send,
            recv_sem=pan_recv.at[j],
            device_id=device,
            device_id_type=MESH,
        ).start()

    def push_all(j):
        dx, dy = twos[j]
        if j:
            push(j, 0, LO, chip(dx, dy))
        push(j, 0, LO // 2, chip(dx, dy, 1))
        push(j, 1, LO // 2, chip(dx, dy, -1))

    other_core = {"list": list_of(zl, y, x, 1 - c), "row": r}

    def arrive(j):
        wait_for(pan.at[pl.ds(0, 2 * LO if j else LO)], pan_recv.at[j])
        here = pl.ds(pl.multiple_of((j * 2 + c) * 2 * LO, 2 * LO), 2 * LO)
        pltpu.make_async_remote_copy(
            src_ref=pan.at[here],
            dst_ref=pan.at[here],
            send_sem=core_send,
            recv_sem=core_recv.at[j],
            device_id=other_core,
            device_id_type=MESH,
        ).start()

    def score(j, first_block, end_block):
        wide = NEXT_DEV
        chunk = pan[j * 4 * LO : (j + 1) * 4 * LO, :]

        def one(b, carry_):
            lanes = pl.ds(pl.multiple_of(b * wide, wide), wide)
            found = nt(chunk, nexts[lanes, :])
            top = jnp.max(found.reshape(4 * LO // 8, 8, wide), axis=0)
            best[:, lanes] = top if j == 0 else jnp.maximum(best[:, lanes], top)
            return carry_

        lax.fori_loop(first_block, end_block, one, 0)

    for j in range(3):
        push_all(j)
    out_cent[...] = centroid
    arrive(0)
    push_all(3)
    away_end, near_end = AWAY // NEXT_DEV, NEAR // NEXT_DEV
    for j in range(4):
        wait_for(pan.at[pl.ds(0, 2 * LO)], core_recv.at[j])
        if j == 0:
            score(0, away_end, near_end)
            for k in range(4, 12):
                wait_for(nexts.at[pl.ds(0, PIECE)], next_recv.at[k])
        score(j, 0, away_end)
        if j < 3:
            arrive(j + 1)
    for j, (dx, dy) in enumerate(((-1, 0), (1, 0), (0, -1), (0, 1), (-1, -1), (1, 1))):
        best_in[j] = jnp.max(best[:, j * HALF : (j + 1) * HALF], axis=0, keepdims=True)
        pltpu.make_async_remote_copy(
            src_ref=best_in.at[j],
            dst_ref=best_in.at[6 + j],
            send_sem=best_sem.at[0],
            recv_sem=best_sem.at[1],
            device_id=chip(dx, dy),
            device_id_type=MESH,
        ).start()
    for j in range(1, 4):
        score(j, away_end, near_end)
    top_own = jnp.max(best[:, AWAY:], axis=0, keepdims=True)

    wait_for(ids_send.at[pl.ds(0, N_LIST - 1)], ids_send_sem)
    wait_for(send.at[pl.ds(0, (N_LIST - 1) * CAP2)], a2a_send)
    wait_for(nexts.at[pl.ds(0, 12 * PIECE)], next_send)
    wait_for(first_high.at[three], high_sem.at[0])
    wait_for(first_low.at[three], low_sem.at[0])
    for step in range(ITERS):
        wait_for(direction.at[step].at[three], dir_sem.at[2 * step])
    for step in range(ITERS - 1):
        wait_for(grams.at[step].at[three], gram_sem.at[2 * step])
    wait_for(last.at[three], last_sem.at[0])
    wait_for(dots_in.at[pl.ds(0, N_ROW - 1)], dot_sem.at[0])
    wait_for(pan.at[pl.ds(0, 7 * LO)], pan_send)
    wait_for(pan.at[pl.ds(0, 8 * LO)], core_send)
    wait_for(best_in.at[pl.ds(0, 6)], best_sem.at[0])
    wait_for(best_in.at[pl.ds(0, 6)], best_sem.at[1])
    for h in range(2):
        top = top_own[:, h * HALF : (h + 1) * HALF]
        for k in range(3):
            top = jnp.maximum(top, best_in[6 + 2 * k + h])
        out_best[:, h * HALF : (h + 1) * HALF] = top / D


def on_device(corpus, row_list, list_slot, member_counts, old_centroids, next_rows):
    vmem = pl.BlockSpec(memory_space=pltpu.VMEM)
    hbm = pl.BlockSpec(memory_space=pl.ANY)
    dma = pltpu.SemaphoreType.DMA
    cent, best = pl.pallas_call(
        kernel,
        out_shape=(
            jax.ShapeDtypeStruct((LO, D), F32),
            jax.ShapeDtypeStruct((1, NEXT_DEV), F32),
        ),
        in_specs=[hbm, vmem, vmem, vmem, vmem, hbm],
        out_specs=(vmem, vmem),
        scratch_shapes=[
            pltpu.VMEM((ROWS_DEV, D), BF16),
            pltpu.VMEM((N_LIST, ROWS_DEV), I32),
            pltpu.VMEM((N_LIST, 128), F32),
            pltpu.VMEM((N_LIST * CAP2, H), BF16),
            pltpu.VMEM((N_LIST, 128), F32),
            pltpu.VMEM((N_LIST * CAP2, H), BF16),
            pltpu.VMEM((N_LIST * CAP, D), BF16),
            pltpu.VMEM((LO, N_LIST * CAP), F32),
            pltpu.VMEM((LO, D), F32),
            pltpu.VMEM((LO, D), BF16),
            pltpu.VMEM((LO, D), BF16),
            pltpu.VMEM((LO, D), BF16),
            pltpu.VMEM((LO, D), BF16),
            pltpu.VMEM((LO, D), F32),
            pltpu.VMEM((ITERS, LO, D), BF16),
            pltpu.VMEM((ITERS - 1, LO, D), BF16),
            pltpu.VMEM((ITERS - 1, LO, D), BF16),
            pltpu.VMEM((LO, D + 128), F32),
            pltpu.VMEM((N_ROW, 128), F32),
            pltpu.VMEM((LO, 128), F32),
            pltpu.VMEM((SHARDS * LO, D), BF16),
            pltpu.VMEM((NEAR, D), BF16),
            pltpu.VMEM((8, NEAR), F32),
            pltpu.VMEM((12, 1, HALF), F32),
            dma, dma, dma((4,)), dma, dma((4,)),
            dma((2,)), dma((2,)), dma((2 * ITERS,)), dma((2 * ITERS - 2,)), dma((2,)), dma((2,)),
            dma, dma, dma((12,)), dma, dma((4,)), dma, dma((4,)), dma((2,)),
        ],
        compiler_params=pltpu.CompilerParams(
            collective_id=0, has_side_effects=True, vmem_limit_bytes=56 * 2**20
        ),
    )(
        corpus,
        row_list.reshape(1, ROWS_DEV),
        list_slot.reshape(32, 128),
        member_counts.reshape(1, LO),
        old_centroids,
        next_rows,
    )
    return cent, best.reshape(NEXT_DEV)


def solution(mesh):
    in_specs = (
        P(("list", "row"), None),
        P(("list", "row")),
        P(),
        P("list"),
        P("list", None),
        P(("list", "row"), None),
    )
    out_specs = (P("list", None), P(("list", "row")))
    return jax.shard_map(
        on_device, mesh=mesh, in_specs=in_specs, out_specs=out_specs, check_vma=False
    )
```

time: 131 us -> 116 us (0.89)
  Pallas kernels: 127 us -> 112 us
    pallas_call x1, Pallas kernels: 127 us -> 112 us  [on_device(): pl.pallas_call(kernel, out_shape=(jax.ShapeDtypeStruct((LO, D), F32), jax...]
where the time goes in v2:
time: 116 us
  Pallas kernels  112 us (97%)
  local copies, waits for them, and re-layouts  1.62 us (1%)
  other arithmetic  1.31 us (1%)
    pallas_call x1, Pallas kernels, on_device(): pl.pallas_call(kernel, out_shape=(jax.ShapeDtypeStruct((LO, D), F32), jax...  112 us

profile of v2, /device:TPU:1, one launch (start us, length us, event | category | flops | bytes accessed | tf_op | source)
XLA Modules:
  0.0 115.8 jit_solution(14879497186599785265)
XLA Ops:
  0.6 112.2 %shard_map.77 = (f32[64,768]{1,0:T(8,128)}, f32[1,1536]{1,0:T(1,128)}) custom-call(bf16[1024,768]{1,0:T(8,128)(2,1)} %corpus_hbm.1, s32[1,1024]{1,0:T(1,128)} %bitcast.4, s32[32,128]{1,0:T(8,128)} %bitcast.3, s32[1,64]{1,0:T(1,128)} %bitcast.5, f32[64,768]{1,0:T(8,128)} %old.1, bf16[1536,768]{1,0:T(8,128)(2,1)} %next_hbm.1), custom_call_target="tpu_custom_call" | custom-call | tf_op jit(solution)/shard_map/pallas_call | solution.py:497
  112.9 1.3 %reduce = f32[1536]{0:T(1024)} reduce(f32[1,1536]{1,0:T(1,128)} %get-tuple-element.5, f32[]{:T(128)} %constant), dimensions={0}, to_apply=%get-tuple-element.5.reduce_sub_computation | reduce | bytes 12292 | tf_op jit(solution)/shard_map/pallas_call | solution.py:497
  114.2 1.6 %copy.9 = f32[64,768]{1,0:T(8,128)} copy(f32[64,768]{1,0:T(8,128)} %get-tuple-element.8) | data formatting | bytes 393216

commit v3 on v2

--- a/solution.py
+++ b/solution.py
@@ -157,10 +157,8 @@
     ids_send[...] = nt(named, at_rank) - 1.0
 
     own_corpus.wait()
-    pl.semaphore_wait(barrier, N_LIST - 1 + N_ROW - 1 + 8)
-
-    def send_group(chunk, carry_):
-        group = (mine + chunk) % 4
+
+    def fill_group(group, carry_):
         keys = key[pl.ds(pl.multiple_of(group * GROUP, GROUP), GROUP), :]
         chosen = keys.reshape(GROUP, 1, ROWS_DEV) == iota((GROUP, CAP, ROWS_DEV), 1)
         chosen = chosen.astype(F32).reshape(GROUP * CAP, ROWS_DEV).astype(BF16)
@@ -169,6 +167,13 @@
         send[pl.ds(pl.multiple_of(group * GROUP * CAP2, GROUP * CAP2), GROUP * CAP2), :] = (
             rows.reshape(GROUP * CAP2, H).astype(BF16)
         )
+        return carry_
+
+    lax.fori_loop(0, 4, fill_group, 0)
+    pl.semaphore_wait(barrier, N_LIST - 1 + N_ROW - 1 + 8)
+
+    def send_group(chunk):
+        group = (mine + chunk) % 4
 
         def send_one(to, device):
             pltpu.make_async_remote_copy(
@@ -202,9 +207,11 @@
                     else:
                         pl.when(chunk > 0)(lambda to=to, device=device: send_one(to, device))
 
+    def send_next(chunk, carry_):
+        send_group(chunk)
         return carry_
 
-    lax.fori_loop(0, 4, send_group, 0)
+    lax.fori_loop(0, 4, send_next, 0)
     own_block = pl.ds(pl.multiple_of(place * CAP2, CAP2), CAP2)
     recv[own_block, :] = send[own_block, :]
     ids_recv[pl.ds(place, 1), :] = ids_send[pl.ds(place, 1), :]
@@ -289,7 +296,7 @@
         return pl.ds(pl.multiple_of(peer(k) * QUARTER, QUARTER), QUARTER)
 
     def scatter(source, target, send_sem, recv_sem):
-        for k in (1, 3, 2):
+        for k in (2, 1, 3):
             pltpu.make_async_remote_copy(
                 src_ref=source.at[rows_of(k)],
                 dst_ref=target.at[quarter],
@@ -300,7 +307,7 @@
             ).start()
 
     def gather(ref, send_sem, recv_sem):
-        for k in (1, 3, 2):
+        for k in (2, 1, 3):
             pltpu.make_async_remote_copy(
                 src_ref=ref.at[quarter],
                 dst_ref=ref.at[quarter],
@@ -392,13 +399,14 @@
     step_len = last[:, D : D + 1] / (bend + gram_weight * total)
     centroid = last[:, :D] + step_len * moved
 
-    own_rows = pl.ds(pl.multiple_of((c * 2 + zl) * LO, LO), LO)
-    pan[own_rows, :] = centroid.astype(BF16)
+    def pan_rows(start, n):
+        return pl.ds(pl.multiple_of(start, n), n)
 
     def push(j, part, n, device):
+        start = ((j * 2 + c) * 2 + zl) * LO if j else 2 * LO + c * LO
         pltpu.make_async_remote_copy(
-            src_ref=pan.at[pl.ds(pl.multiple_of((c * 2 + zl) * LO + part * n, n), n)],
-            dst_ref=pan.at[pl.ds(pl.multiple_of(((j * 2 + c) * 2 + zl) * LO + part * n, n), n)],
+            src_ref=pan.at[pan_rows(c * LO + part * n, n)],
+            dst_ref=pan.at[pan_rows(start + part * n, n)],
             send_sem=pan_send,
             recv_sem=pan_recv.at[j],
             device_id=device,
@@ -414,46 +422,54 @@
 
     other_core = {"list": list_of(zl, y, x, 1 - c), "row": r}
 
-    def arrive(j):
-        wait_for(pan.at[pl.ds(0, 2 * LO if j else LO)], pan_recv.at[j])
-        here = pl.ds(pl.multiple_of((j * 2 + c) * 2 * LO, 2 * LO), 2 * LO)
+    def share(rows, at):
         pltpu.make_async_remote_copy(
-            src_ref=pan.at[here],
-            dst_ref=pan.at[here],
+            src_ref=pan.at[rows],
+            dst_ref=pan.at[rows],
             send_sem=core_send,
-            recv_sem=core_recv.at[j],
+            recv_sem=core_recv.at[at],
             device_id=other_core,
             device_id_type=MESH,
         ).start()
 
-    def score(j, first_block, end_block):
+    def arrive(j):
+        n = 2 * LO if j else LO
+        wait_for(pan.at[pl.ds(0, n)], pan_recv.at[j])
+        share(pan_rows((j * 2 + c) * 2 * LO if j else 2 * LO + c * LO, n), j)
+
+    def score(chunk, first_block, end_block):
+        start, end = chunk
         wide = NEXT_DEV
-        chunk = pan[j * 4 * LO : (j + 1) * 4 * LO, :]
+        lists = pan[start:end, :]
 
         def one(b, carry_):
             lanes = pl.ds(pl.multiple_of(b * wide, wide), wide)
-            found = nt(chunk, nexts[lanes, :])
-            top = jnp.max(found.reshape(4 * LO // 8, 8, wide), axis=0)
-            best[:, lanes] = top if j == 0 else jnp.maximum(best[:, lanes], top)
+            found = nt(lists, nexts[lanes, :])
+            top = jnp.max(found.reshape((end - start) // 8, 8, wide), axis=0)
+            best[:, lanes] = jnp.maximum(best[:, lanes], top) if start else top
             return carry_
 
         lax.fori_loop(first_block, end_block, one, 0)
 
-    for j in range(3):
+    own_rows = pan_rows(c * LO, LO)
+    pan[own_rows, :] = centroid.astype(BF16)
+    share(own_rows, 4)
+    for j in range(4):
         push_all(j)
     out_cent[...] = centroid
+    away_end, near_end = AWAY // NEXT_DEV, NEAR // NEXT_DEV
+    chunks = ((0, 2 * LO), (2 * LO, 8 * LO), (8 * LO, 12 * LO), (12 * LO, 16 * LO))
+    wait_for(pan.at[pl.ds(0, LO)], core_recv.at[4])
+    score(chunks[0], away_end, near_end)
     arrive(0)
-    push_all(3)
-    away_end, near_end = AWAY // NEXT_DEV, NEAR // NEXT_DEV
-    for j in range(4):
+    for k in range(4, 12):
+        wait_for(nexts.at[pl.ds(0, PIECE)], next_recv.at[k])
+    score(chunks[0], 0, away_end)
+    wait_for(pan.at[pl.ds(0, LO)], core_recv.at[0])
+    for j in range(1, 4):
+        arrive(j)
         wait_for(pan.at[pl.ds(0, 2 * LO)], core_recv.at[j])
-        if j == 0:
-            score(0, away_end, near_end)
-            for k in range(4, 12):
-                wait_for(nexts.at[pl.ds(0, PIECE)], next_recv.at[k])
-        score(j, 0, away_end)
-        if j < 3:
-            arrive(j + 1)
+        score(chunks[j], 0, away_end)
     for j, (dx, dy) in enumerate(((-1, 0), (1, 0), (0, -1), (0, 1), (-1, -1), (1, 1))):
         best_in[j] = jnp.max(best[:, j * HALF : (j + 1) * HALF], axis=0, keepdims=True)
         pltpu.make_async_remote_copy(
@@ -465,7 +481,7 @@
             device_id_type=MESH,
         ).start()
     for j in range(1, 4):
-        score(j, away_end, near_end)
+        score(chunks[j], away_end, near_end)
     top_own = jnp.max(best[:, AWAY:], axis=0, keepdims=True)
 
     wait_for(ids_send.at[pl.ds(0, N_LIST - 1)], ids_send_sem)
@@ -487,7 +503,12 @@
         top = top_own[:, h * HALF : (h + 1) * HALF]
         for k in range(3):
             top = jnp.maximum(top, best_in[6 + 2 * k + h])
-        out_best[:, h * HALF : (h + 1) * HALF] = top / D
+        out_best[:, h * HALF : (h + 1) * HALF] = top
+
+
+def finish(cent, best, out_cent, out_best):
+    out_cent[...] = cent[...]
+    out_best[...] = best[...].reshape(NEXT_DEV) / D
 
 
 def on_device(corpus, row_list, list_slot, member_counts, old_centroids, next_rows):
@@ -529,7 +550,7 @@
             pltpu.VMEM((12, 1, HALF), F32),
             dma, dma, dma((4,)), dma, dma((4,)),
             dma((2,)), dma((2,)), dma((2 * ITERS,)), dma((2 * ITERS - 2,)), dma((2,)), dma((2,)),
-            dma, dma, dma((12,)), dma, dma((4,)), dma, dma((4,)), dma((2,)),
+            dma, dma, dma((12,)), dma, dma((4,)), dma, dma((5,)), dma((2,)),
         ],
         compiler_params=pltpu.CompilerParams(
             collective_id=0, has_side_effects=True, vmem_limit_bytes=56 * 2**20
@@ -542,7 +563,15 @@
         old_centroids,
         next_rows,
     )
-    return cent, best.reshape(NEXT_DEV)
+    return pl.pallas_call(
+        finish,
+        out_shape=(
+            jax.ShapeDtypeStruct((LO, D), F32),
+            jax.ShapeDtypeStruct((NEXT_DEV,), F32),
+        ),
+        in_specs=[vmem, vmem],
+        out_specs=(vmem, vmem),
+    )(cent, best)
 
 
 def solution(mesh):

time: 116 us -> 115 us (level)
  Pallas kernels: 112 us -> 114 us
  local copies, waits for them, and re-layouts: 1.62 us -> 0 us
  other arithmetic: 1.31 us -> 0 us
    pallas_call x0 -> x1, Pallas kernels: none -> 1.62 us  [on_device(): pl.pallas_call(finish, out_shape=(jax.ShapeDtypeStruct((LO, D), F32), jax...]
    unnamed x1 -> x0, local copies, waits for them, and re-layouts: 1.62 us -> none
    pallas_call x1 -> x0, other arithmetic: 1.31 us -> none  [on_device(): pl.pallas_call(kernel, out_shape=(jax.ShapeDtypeStruct((LO, D), F32), jax...]
where the time goes in v3:
time: 115 us; the launch traced here: 114 us
  Pallas kernels  114 us (99%)
    pallas_call x1, Pallas kernels, on_device(): pl.pallas_call(kernel, out_shape=(jax.ShapeDtypeStruct((LO, D), F32), jax...  112 us

profile of v3, /device:TPU:1, one launch (start us, length us, event | category | flops | bytes accessed | tf_op | source)
XLA Modules:
  0.0 114.4 jit_solution(11018086061475817057)
XLA Ops:
  0.6 112.2 %shard_map.77 = (f32[64,768]{1,0:T(8,128)}, f32[1,1536]{1,0:T(1,128)}) custom-call(bf16[1024,768]{1,0:T(8,128)(2,1)} %corpus_hbm.1, s32[1,1024]{1,0:T(1,128)} %bitcast.4, s32[32,128]{1,0:T(8,128)} %bitcast.3, s32[1,64]{1,0:T(1,128)} %bitcast.5, f32[64,768]{1,0:T(8,128)} %old.1, bf16[1536,768]{1,0:T(8,128)(2,1)} %next_hbm.1), custom_call_target="tpu_custom_call" | custom-call | tf_op jit(solution)/shard_map/pallas_call | solution.py:518
  112.8 1.6 %shard_map.78 = (f32[64,768]{1,0:T(8,128)}, f32[1536]{0:T(1024)}) custom-call(f32[64,768]{1,0:T(8,128)} %get-tuple-element.4.cent, f32[1,1536]{1,0:T(1,128)} %get-tuple-element.5.best), custom_call_target="tpu_custom_call" | custom-call | tf_op jit(solution)/shard_map/pallas_call | solution.py:566

commit v4 on v3

--- a/solution.py
+++ b/solution.py
@@ -109,8 +109,7 @@
     for k in (2, 1, 3):
         greet_device({"list": l, "row": (r + k) % N_ROW})
     for dx, dy in twos[::-1]:
-        for dz in (1, -1):
-            greet_device(chip(dx, dy, dz))
+        greet_device({"list": list_of(1 - zl, (y + dy) % 4, (x + dx) % 4, c), "row": row_core[1]})
     offsets = itertools.product(range(4), range(4), range(2), range(2))
     for dy, dx, dz, dc in sorted(offsets, key=lambda o: -RING[o[0]] - RING[o[1]] - o[2]):
         if dy or dx or dz or dc:
@@ -170,7 +169,7 @@
         return carry_
 
     lax.fori_loop(0, 4, fill_group, 0)
-    pl.semaphore_wait(barrier, N_LIST - 1 + N_ROW - 1 + 8)
+    pl.semaphore_wait(barrier, N_LIST - 1 + N_ROW - 1 + len(twos))
 
     def send_group(chunk):
         group = (mine + chunk) % 4
@@ -244,21 +243,21 @@
     def take_group(chunk, carry_):
         group = (mine - chunk + 4) % 4
 
-        @pl.when(chunk == 0)
-        def _():
-            wait_for(ids_recv.at[pl.ds(0, GROUP - 1)], ids_recv_sem.at[0])
-            wait_for(recv.at[pl.ds(0, (GROUP - 1) * CAP2)], a2a_recv.at[0])
-
-        @pl.when(chunk > 0)
-        def _():
-            wait_for(ids_recv.at[pl.ds(0, GROUP)], ids_recv_sem.at[chunk])
-            wait_for(recv.at[pl.ds(0, GROUP * CAP2)], a2a_recv.at[chunk])
-
         @pl.when(chunk == 3)
         def _():
             own_next.wait()
             for j, (dx, dy) in enumerate(sides):
                 pass_on(AWAY + (j % 2) * HALF + (j // 2) * PIECE, j, j // 2, chip(dx, dy), j)
+
+        @pl.when(chunk == 0)
+        def _():
+            wait_for(ids_recv.at[pl.ds(0, GROUP - 1)], ids_recv_sem.at[0])
+            wait_for(recv.at[pl.ds(0, (GROUP - 1) * CAP2)], a2a_recv.at[0])
+
+        @pl.when(chunk > 0)
+        def _():
+            wait_for(ids_recv.at[pl.ds(0, GROUP)], ids_recv_sem.at[chunk])
+            wait_for(recv.at[pl.ds(0, GROUP * CAP2)], a2a_recv.at[chunk])
 
         named_in = ids_recv[pl.ds(pl.multiple_of(group * GROUP, GROUP), GROUP), :]
         wide = nn(named_in.astype(BF16), spread)
@@ -319,27 +318,30 @@
 
     three = pl.ds(0, 3 * QUARTER)
 
-    def pass_more():
+    def pass_rest():
+        for j, (dx, dy) in enumerate(sides):
+            part = 1 - j // 2
+            pass_on(AWAY + (j % 2) * HALF + part * PIECE, j, part, chip(dx, dy), 4 + j)
+
+    def pass_over():
         for j in range(4):
             wait_for(nexts.at[pl.ds(0, PIECE)], next_recv.at[j])
         for j, (dx, dy) in enumerate(sides):
             part = j // 2
-            over = chip(dy, dx)
-            pass_on(j * HALF + part * PIECE, 4 + j % 2, part, over, 8 + j)
-            pass_on(AWAY + (j % 2) * HALF + (1 - part) * PIECE, j, 1 - part, chip(dx, dy), 4 + j)
+            pass_on(j * HALF + part * PIECE, 4 + j % 2, part, chip(dy, dx), 8 + j)
 
     high_part, low_part = split_pair(first[...])
     first_high[...] = high_part
     first_low[...] = low_part
     scatter(first_high, high_in, high_sem.at[0], high_sem.at[1])
-    scatter(first_low, low_in, low_sem.at[0], low_sem.at[1])
     old_own = old[quarter, :]
     diag_own = diag[quarter, :][:, :1]
     residual = first[quarter, :] + (prior_weight - diag_own) * old_own
     wait_for(high_in.at[three], high_sem.at[1])
+    pass_rest()
     for k in range(1, N_ROW):
         residual = residual + high_in[rows_of(k), :].astype(F32)
-    centroid = old_own
+    step_lens = []
     moved = residual
     for step in range(ITERS):
         dir_now = direction.at[step]
@@ -347,10 +349,14 @@
         moved = moved.astype(BF16).astype(F32)
         gather(dir_now, dir_sem.at[2 * step], dir_sem.at[2 * step + 1])
         if step == ITERS - 1:
-            last[quarter, :D] = centroid
-            last[quarter, D:] = jnp.broadcast_to(norm_now, (QUARTER, 128))
+            lane = iota((QUARTER, 128), 1)
+            last[quarter, :] = jnp.where(
+                lane == 0, step_lens[0], jnp.where(lane == 1, step_lens[1], norm_now)
+            )
             gather(last, last_sem.at[0], last_sem.at[1])
         wait_for(dir_now.at[three], dir_sem.at[2 * step + 1])
+        if step == 0:
+            scatter(first_low, low_in, low_sem.at[0], low_sem.at[1])
         scores = nt(dir_now[...], unit[...]) * member[...]
         if step == ITERS - 1:
             break
@@ -361,7 +367,7 @@
             grams.at[step], grams_in.at[step], gram_sem.at[2 * step], gram_sem.at[2 * step + 1]
         )
         if step == 0:
-            pass_more()
+            pass_over()
             wait_for(low_in.at[three], low_sem.at[1])
             for k in range(1, N_ROW):
                 residual = residual + low_in[rows_of(k), :].astype(F32)
@@ -372,7 +378,7 @@
             total = total + grams_in.at[step][rows_of(k), :].astype(F32)
         applied = diag_own * moved + gram_weight * total
         step_len = norm_now / jnp.sum(moved * applied, axis=1, keepdims=True)
-        centroid = centroid + step_len * moved
+        step_lens.append(step_len)
         residual = residual - step_len * applied
         norm_next = jnp.sum(residual * residual, axis=1, keepdims=True)
         moved = residual + norm_next / norm_now * moved
@@ -396,8 +402,11 @@
     wait_for(dots_in.at[pl.ds(0, N_ROW - 1)], dot_sem.at[1])
     total = jnp.sum(dots_in[...], axis=0, keepdims=True)[:, :LO]
     total = jnp.sum(jnp.where(square, total, 0.0), axis=1, keepdims=True)
-    step_len = last[:, D : D + 1] / (bend + gram_weight * total)
-    centroid = last[:, :D] + step_len * moved
+    step_len = last[:, 2:3] / (bend + gram_weight * total)
+    centroid = old[...]
+    for step in range(ITERS - 1):
+        centroid = centroid + last[:, step : step + 1] * direction[step].astype(F32)
+    centroid = centroid + step_len * moved
 
     def pan_rows(start, n):
         return pl.ds(pl.multiple_of(start, n), n)
@@ -541,7 +550,7 @@
             pltpu.VMEM((ITERS, LO, D), BF16),
             pltpu.VMEM((ITERS - 1, LO, D), BF16),
             pltpu.VMEM((ITERS - 1, LO, D), BF16),
-            pltpu.VMEM((LO, D + 128), F32),
+            pltpu.VMEM((LO, 128), F32),
             pltpu.VMEM((N_ROW, 128), F32),
             pltpu.VMEM((LO, 128), F32),
             pltpu.VMEM((SHARDS * LO, D), BF16),

time: 115 us -> 111 us (0.965)
  Pallas kernels: 114 us -> 110 us
    pallas_call x1, Pallas kernels: 112 us -> 109 us  [on_device(): pl.pallas_call(kernel, out_shape=(jax.ShapeDtypeStruct((LO, D), F32), jax...]
where the time goes in v4:
time: 111 us
  Pallas kernels  110 us (99%)
    pallas_call x1, Pallas kernels, on_device(): pl.pallas_call(kernel, out_shape=(jax.ShapeDtypeStruct((LO, D), F32), jax...  109 us

profile of v4, /device:TPU:1, one launch (start us, length us, event | category | flops | bytes accessed | tf_op | source)
XLA Modules:
  0.0 110.9 jit_solution(3147771494857260024)
XLA Ops:
  0.6 108.6 %shard_map.77 = (f32[64,768]{1,0:T(8,128)}, f32[1,1536]{1,0:T(1,128)}) custom-call(bf16[1024,768]{1,0:T(8,128)(2,1)} %corpus_hbm.1, s32[1,1024]{1,0:T(1,128)} %bitcast.4, s32[32,128]{1,0:T(8,128)} %bitcast.3, s32[1,64]{1,0:T(1,128)} %bitcast.5, f32[64,768]{1,0:T(8,128)} %old.1, bf16[1536,768]{1,0:T(8,128)(2,1)} %next_hbm.1), custom_call_target="tpu_custom_call" | custom-call | tf_op jit(solution)/shard_map/pallas_call | solution.py:527
  109.3 1.6 %shard_map.78 = (f32[64,768]{1,0:T(8,128)}, f32[1536]{0:T(1024)}) custom-call(f32[64,768]{1,0:T(8,128)} %get-tuple-element.4.cent, f32[1,1536]{1,0:T(1,128)} %get-tuple-element.5.best), custom_call_target="tpu_custom_call" | custom-call | tf_op jit(solution)/shard_map/pallas_call | solution.py:575

commit v5 on v4

--- a/solution.py
+++ b/solution.py
@@ -243,7 +243,7 @@
     def take_group(chunk, carry_):
         group = (mine - chunk + 4) % 4
 
-        @pl.when(chunk == 3)
+        @pl.when(chunk == 2)
         def _():
             own_next.wait()
             for j, (dx, dy) in enumerate(sides):

time: 111 us -> 109 us (0.982)
  Pallas kernels: 110 us -> 108 us
    pallas_call x1, Pallas kernels: 109 us -> 107 us  [on_device(): pl.pallas_call(kernel, out_shape=(jax.ShapeDtypeStruct((LO, D), F32), jax...]
where the time goes in v5:
time: 109 us
  Pallas kernels  108 us (99%)
    pallas_call x1, Pallas kernels, on_device(): pl.pallas_call(kernel, out_shape=(jax.ShapeDtypeStruct((LO, D), F32), jax...  107 us

profile of v5, /device:TPU:1, one launch (start us, length us, event | category | flops | bytes accessed | tf_op | source)
XLA Modules:
  0.0 108.8 jit_solution(5357158641652237815)
XLA Ops:
  0.6 106.5 %shard_map.77 = (f32[64,768]{1,0:T(8,128)}, f32[1,1536]{1,0:T(1,128)}) custom-call(bf16[1024,768]{1,0:T(8,128)(2,1)} %corpus_hbm.1, s32[1,1024]{1,0:T(1,128)} %bitcast.4, s32[32,128]{1,0:T(8,128)} %bitcast.3, s32[1,64]{1,0:T(1,128)} %bitcast.5, f32[64,768]{1,0:T(8,128)} %old.1, bf16[1536,768]{1,0:T(8,128)(2,1)} %next_hbm.1), custom_call_target="tpu_custom_call" | custom-call | tf_op jit(solution)/shard_map/pallas_call | solution.py:527
  107.2 1.6 %shard_map.78 = (f32[64,768]{1,0:T(8,128)}, f32[1536]{0:T(1024)}) custom-call(f32[64,768]{1,0:T(8,128)} %get-tuple-element.4.cent, f32[1,1536]{1,0:T(1,128)} %get-tuple-element.5.best), custom_call_target="tpu_custom_call" | custom-call | tf_op jit(solution)/shard_map/pallas_call | solution.py:575
